TPU v7x, 512 devices: a whole 4x8x8 slice. The times are simulated.
512 devices in a mesh: src: 8 (over x, y_lo), gx: 16 (over z, core), gy: 4 (over y_hi).
Axes of the slice: x: 4, y: 8 (y_hi: 4, y_lo: 2; y = y_hi * 2 + y_lo), z: 8, core: 2. Of those that a mesh axis runs over, the one named last changes fastest.
Arguments:
- warm_potential: float32 [32, 64, 128, 128], P('src', 'gx', 'gy'), may hold values from -3 to 3
- warm_adjoint: float32 [32, 64, 128, 128], P('src', 'gx', 'gy'), may hold values from -3 to 3
- conductivity: float32 [64, 128, 128], P('gx', 'gy', 'src'), may hold values from 0.2 to 5
- electrodes: int32 [32, 2], replicated, may hold values from 0 to 8191
- receivers: int32 [128, 2], replicated, may hold values from 0 to 8191
- observed: float32 [32, 128], replicated, may hold values from -6 to 6
- source_order: int32 [32], replicated, may hold values from 0 to 31, each once
Outputs:
- gradient: float32 [64, 128, 128], P('gx', 'gy', 'src')
Inputs may be any that keep to these rules, and one draw needn't show every extreme that they name: `electrodes`: entries number surface cells as x * 128 + y. `receivers`: entries number surface cells as x * 128 + y.
All inputs are finite; a program needn't handle non-finite values.
Results may differ from a plain program's by a relative error of at most 0.0003.
Values sent between devices are 32-bit elements; how exact they have to be, the bound alone decides.
A program may use at most 64 MiB of HBM per device.

v0:
```python
import jax
import jax.numpy as jnp
from jax import lax
from jax.sharding import PartitionSpec as P

SWEEPS = 6
lowest = 0.05
highest = 2.0
centre = (highest + lowest) / 2.0
half_span = (highest - lowest) / 2.0
bound_ratio = centre / half_span
strength = 4.0


def padded_2(block, sides, width):
    for axis, dim in sides:
        count = lax.axis_size(axis)
        forward = [(i, i + 1) for i in range(count - 1)]
        backward = [(target, source) for source, target in forward]
        low = lax.ppermute(
            lax.slice_in_dim(block, block.shape[dim] - width, None, axis=dim), axis, forward
        )
        high = lax.ppermute(lax.slice_in_dim(block, 0, width, axis=dim), axis, backward)
        block = jnp.concatenate([low, block, high], axis=dim)
    return block


def harmonic(left, right):
    return jnp.where(right > 0, 2.0 * left * right / (left + right), left)


def slope_of(left, right):
    total = left + right
    return jnp.where(right > 0, 2.0 * right * right / (total * total), 1.0)


def neighbours(field, padded):
    widths = [(0, 0)] * (field.ndim - 1) + [(1, 1)]
    deeper = jnp.pad(field, widths)
    return (
        padded[..., :-2, 1:-1, :],
        padded[..., 2:, 1:-1, :],
        padded[..., 1:-1, :-2, :],
        padded[..., 1:-1, 2:, :],
        deeper[..., :-2],
        deeper[..., 2:],
    )


def face_tables(sigma, padded):
    others = neighbours(sigma, padded)
    depth = lax.broadcasted_iota(jnp.int32, sigma.shape, 2)
    surface = depth == 0
    coeffs = [harmonic(sigma, other) for other in others]
    slopes = [slope_of(sigma, other) for other in others]
    coeffs[4] = jnp.where(surface, 0.0, coeffs[4])
    slopes[4] = jnp.where(surface, 0.0, slopes[4])
    return (coeffs, slopes)


def apply_operator(field, padded, coeffs):
    others = neighbours(field, padded)
    total = coeffs[0] * (field - others[0])
    for index in range(1, 6):
        total = total + coeffs[index] * (field - others[index])
    return total


def solve(rhs, start, coeffs, inverse, pad_fn):
    residual = rhs - apply_operator(start, pad_fn(start), coeffs)
    update = inverse * residual / centre
    iterate = start
    factor = 1.0 / bound_ratio
    for sweep in range(SWEEPS):
        iterate = iterate + update
        residual = residual - apply_operator(update, pad_fn(update), coeffs)
        following = 1.0 / (2.0 * bound_ratio - factor)
        update = following * factor * update + 2.0 * following / half_span * (inverse * residual)
        factor = following
    return iterate + update


def gradient_term(potential, adjoint, padded_potential, padded_adjoint, slopes):
    near_potential = neighbours(potential, padded_potential)
    near_adjoint = neighbours(adjoint, padded_adjoint)
    total = slopes[0] * (potential - near_potential[0]) * (adjoint - near_adjoint[0])
    for index in range(1, 6):
        total = total + slopes[index] * (potential - near_potential[index]) * (
            adjoint - near_adjoint[index]
        )
    return total


def pad_joint(field):
    return padded_2(field, (("gx", 1), ("gy", 2)), 1)


def reduce_groups(partial_value, depth):
    summed = lax.psum(partial_value, "src")
    return lax.dynamic_slice_in_dim(summed, lax.axis_index("src") * depth, depth, 2)


def body(warm_potential, warm_adjoint, conductivity, electrodes, receivers, observed, source_order):
    panel = lax.all_gather(conductivity, "src", axis=2, tiled=True)
    group = lax.axis_index("src")
    slots = warm_potential.shape[0]
    width_x = panel.shape[0]
    ny_global = panel.shape[1] * lax.axis_size("gy")
    x_start = lax.axis_index("gx") * width_x
    potential_start, adjoint_start = (warm_potential, warm_adjoint)
    first_slot = group * slots
    y_start = lax.axis_index("gy") * panel.shape[1]
    width_y = panel.shape[1]
    depth_cells = panel.shape[2]
    coeffs, slopes = face_tables(panel, pad_joint(panel[None])[0])
    inverse = 1.0 / (coeffs[0] + coeffs[1] + coeffs[2] + coeffs[3] + coeffs[4] + coeffs[5])
    idents = lax.dynamic_slice_in_dim(source_order, first_slot, slots)
    pairs = jnp.take(electrodes, idents, axis=0)
    rows_observed = jnp.take(observed, idents, axis=0)

    def picker(cells):
        local_x = cells // ny_global - x_start
        local_y = cells % ny_global - y_start
        inside = (local_x >= 0) & (local_x < width_x) & (local_y >= 0) & (local_y < width_y)
        flat = local_x * width_y + local_y
        places = lax.broadcasted_iota(jnp.int32, (cells.shape[0], width_x * width_y), 1)
        return jnp.where((flat[:, None] == places) & inside[:, None], 1.0, 0.0).astype(jnp.float32)

    def on_surface(flat):
        field = jnp.zeros((slots, width_x, width_y, depth_cells), jnp.float32)
        return field.at[..., 0].set(flat.reshape(slots, width_x, width_y))

    source_surface = strength * (picker(pairs[:, 0]) - picker(pairs[:, 1]))
    potential = solve(on_surface(source_surface), potential_start, coeffs, inverse, pad_joint)
    pickup = picker(receivers[:, 0]) - picker(receivers[:, 1])
    top = potential[..., 0].reshape(slots, width_x * width_y)
    local_values = jnp.dot(
        top, pickup.T, precision=lax.Precision.HIGHEST, preferred_element_type=jnp.float32
    )
    predicted = lax.psum(local_values, ("gx", "gy"))
    misfit = predicted - rows_observed
    back = jnp.dot(
        misfit, pickup, precision=lax.Precision.HIGHEST, preferred_element_type=jnp.float32
    )
    adjoint = solve(on_surface(back), adjoint_start, coeffs, inverse, pad_joint)
    padded_both = pad_joint(jnp.concatenate([potential, adjoint], 0))
    term = gradient_term(potential, adjoint, padded_both[:slots], padded_both[slots:], slopes)
    partial_value = -jnp.sum(term, axis=0)
    return reduce_groups(partial_value, conductivity.shape[2])


def solution(mesh):
    in_specs = (
        P("src", "gx", "gy", None),
        P("src", "gx", "gy", None),
        P("gx", "gy", "src"),
        P(),
        P(),
        P(),
        P(),
    )
    out_specs = P("gx", "gy", "src")
    return jax.shard_map(body, mesh=mesh, in_specs=in_specs, out_specs=out_specs, check_vma=False)
```

profile of v0, /device:TPU:16, one launch (start us, length us, event | category | flops | bytes accessed | tf_op | source)
XLA Modules:
  0.0 592.4 jit_solution(16727907163246744626)
XLA Ops:
  7.3 29.0 %all_gather.3 = f32[4,32,128]{1,0,2:T(4,128)S(1)} all-gather(f32[4,32,16]{1,0,2:T(4,128)S(1)} %copy.69), channel_id=1, replica_groups=mesh['src'=8,'gx'=16,'gy'=4] {'src'}, dimensions={2}, use_global_device_ids=true | all-gather | bytes 73728 | tf_op jit(solution)/shard_map/all_gather | solution.py:104
  58.0 21.9 %collective-permute-done.3 = f32[1,6,1,128]{2,1,3,0:T(8,128)S(1)} collective-permute-done((f32[1,6,1,128]{2,1,3,0:T(8,128)S(1)}, f32[1,6,1,128]{2,1,3,0:T(8,128)S(1)}, u32[]{:S(2)}, u32[]{:S(2)}) %collective-permute-start.3) | collective-permute-done | bytes 3104 | tf_op jit(solution)/shard_map/ppermute | solution.py:23
  84.7 5.6 collective-permute-start.6
  102.4 6.0 %collective-permute-start.10 = (f32[4,6,1,128]{3,2,1,0:T(1,128)S(1)}, f32[4,6,1,128]{3,2,1,0:T(1,128)S(1)}, u32[]{:S(2)}, u32[]{:S(2)}) collective-permute-start(f32[4,6,1,128]{3,2,1,0:T(1,128)S(1)} %get-tuple-element.118), channel_id=1, source_target_pairs={{0,1},{1,2},{2,3},{4,5},{5,6},{6,7},{8,9},{9,10},{10,11},{12,13},{... | collective-permute-start | bytes 36872 | tf_op jit(solution)/shard_map/ppermute | solution.py:20
  111.4 5.8 collective-permute-start.12
  120.1 6.0 %collective-permute-start.14 = (f32[4,6,1,128]{3,2,1,0:T(1,128)S(1)}, f32[4,6,1,128]{3,2,1,0:T(1,128)S(1)}, u32[]{:S(2)}, u32[]{:S(2)}) collective-permute-start(f32[4,6,1,128]{3,2,1,0:T(1,128)S(1)} %get-tuple-element.116), channel_id=1, source_target_pairs={{0,1},{1,2},{2,3},{4,5},{5,6},{6,7},{8,9},{9,10},{10,11},{12,13},{... | collective-permute-start | bytes 36872 | tf_op jit(solution)/shard_map/ppermute | solution.py:20
  129.3 5.9 collective-permute-start.16
  138.0 6.0 %collective-permute-start.18 = (f32[4,6,1,128]{3,2,1,0:T(1,128)S(1)}, f32[4,6,1,128]{3,2,1,0:T(1,128)S(1)}, u32[]{:S(2)}, u32[]{:S(2)}) collective-permute-start(f32[4,6,1,128]{3,2,1,0:T(1,128)S(1)} %get-tuple-element.114), channel_id=1, source_target_pairs={{0,1},{1,2},{2,3},{4,5},{5,6},{6,7},{8,9},{9,10},{10,11},{12,13},{... | collective-permute-start | bytes 36872 | tf_op jit(solution)/shard_map/ppermute | solution.py:20
  153.2 5.8 collective-permute-start.20
  162.4 6.0 %collective-permute-start.22 = (f32[4,6,1,128]{3,2,1,0:T(1,128)}, f32[4,6,1,128]{3,2,1,0:T(1,128)}, u32[]{:S(2)}, u32[]{:S(2)}) collective-permute-start(f32[4,6,1,128]{3,2,1,0:T(1,128)} %get-tuple-element.112), channel_id=1, source_target_pairs={{0,1},{1,2},{2,3},{4,5},{5,6},{6,7},{8,9},{9,10},{10,11},{12,13},{... | collective-permute-start | bytes 36872 | tf_op jit(solution)/shard_map/ppermute | solution.py:20
  179.5 6.0 %collective-permute-start.26 = (f32[4,6,1,128]{3,2,1,0:T(1,128)S(1)}, f32[4,6,1,128]{3,2,1,0:T(1,128)S(1)}, u32[]{:S(2)}, u32[]{:S(2)}) collective-permute-start(f32[4,6,1,128]{3,2,1,0:T(1,128)S(1)} %get-tuple-element.110), channel_id=1, source_target_pairs={{0,1},{1,2},{2,3},{4,5},{5,6},{6,7},{8,9},{9,10},{10,11},{12,13},{... | collective-permute-start | bytes 36872 | tf_op jit(solution)/shard_map/ppermute | solution.py:20
  196.6 6.0 %collective-permute-start.30 = (f32[4,6,1,128]{3,2,1,0:T(1,128)S(1)}, f32[4,6,1,128]{3,2,1,0:T(1,128)S(1)}, u32[]{:S(2)}, u32[]{:S(2)}) collective-permute-start(f32[4,6,1,128]{3,2,1,0:T(1,128)S(1)} %get-tuple-element.108), channel_id=1, source_target_pairs={{0,1},{1,2},{2,3},{4,5},{5,6},{6,7},{8,9},{9,10},{10,11},{12,13},{... | collective-permute-start | bytes 36872 | tf_op jit(solution)/shard_map/ppermute | solution.py:20
  204.6 6.0 %collective-permute-start.34 = (f32[4,6,1,128]{3,2,1,0:T(1,128)S(1)}, f32[4,6,1,128]{3,2,1,0:T(1,128)S(1)}, u32[]{:S(2)}, u32[]{:S(2)}) collective-permute-start(f32[4,6,1,128]{3,2,1,0:T(1,128)S(1)} %get-tuple-element.106), channel_id=1, source_target_pairs={{0,1},{1,2},{2,3},{4,5},{5,6},{6,7},{8,9},{9,10},{10,11},{12,13},{... | collective-permute-start | bytes 36872 | tf_op jit(solution)/shard_map/ppermute | solution.py:20
  212.4 144.6 %psum.14 = f32[4,128]{1,0:T(4,128)S(1)} all-reduce(f32[4,128]{1,0:T(4,128)S(1)} %fusion.300), channel_id=1, replica_groups=mesh['src'=8,'gx'=16,'gy'=4] {'gx','gy'}, use_global_device_ids=true, to_apply=%region_0.1 | all-reduce | flops 512 | bytes 4096 | tf_op jit(solution)/shard_map/psum | solution.py:140
  382.5 6.0 %collective-permute-start.42 = (f32[4,6,1,128]{3,2,1,0:T(1,128)S(1)}, f32[4,6,1,128]{3,2,1,0:T(1,128)S(1)}, u32[]{:S(2)}, u32[]{:S(2)}) collective-permute-start(f32[4,6,1,128]{3,2,1,0:T(1,128)S(1)} %get-tuple-element.102), channel_id=1, source_target_pairs={{0,1},{1,2},{2,3},{4,5},{5,6},{6,7},{8,9},{9,10},{10,11},{12,13},{... | collective-permute-start | bytes 36872 | tf_op jit(solution)/shard_map/ppermute | solution.py:20
  398.5 6.2 %collective-permute-start.46 = (f32[4,6,1,128]{3,2,1,0:T(1,128)S(1)}, f32[4,6,1,128]{3,2,1,0:T(1,128)S(1)}, u32[]{:S(2)}, u32[]{:S(2)}) collective-permute-start(f32[4,6,1,128]{3,2,1,0:T(1,128)S(1)} %get-tuple-element.100), channel_id=1, source_target_pairs={{0,1},{1,2},{2,3},{4,5},{5,6},{6,7},{8,9},{9,10},{10,11},{12,13},{... | collective-permute-start | bytes 36872 | tf_op jit(solution)/shard_map/ppermute | solution.py:20
  407.5 5.9 collective-permute-start.48
  416.3 6.0 %collective-permute-start.50 = (f32[4,6,1,128]{3,2,1,0:T(1,128)S(1)}, f32[4,6,1,128]{3,2,1,0:T(1,128)S(1)}, u32[]{:S(2)}, u32[]{:S(2)}) collective-permute-start(f32[4,6,1,128]{3,2,1,0:T(1,128)S(1)} %get-tuple-element.98), channel_id=1, source_target_pairs={{0,1},{1,2},{2,3},{4,5},{5,6},{6,7},{8,9},{9,10},{10,11},{12,13},{... | collective-permute-start | bytes 36872 | tf_op jit(solution)/shard_map/ppermute | solution.py:20
  425.3 5.6 collective-permute-start.52
  433.7 6.0 %collective-permute-start.54 = (f32[4,6,1,128]{3,2,1,0:T(1,128)S(1)}, f32[4,6,1,128]{3,2,1,0:T(1,128)S(1)}, u32[]{:S(2)}, u32[]{:S(2)}) collective-permute-start(f32[4,6,1,128]{3,2,1,0:T(1,128)S(1)} %get-tuple-element.96), channel_id=1, source_target_pairs={{0,1},{1,2},{2,3},{4,5},{5,6},{6,7},{8,9},{9,10},{10,11},{12,13},{... | collective-permute-start | bytes 36872 | tf_op jit(solution)/shard_map/ppermute | solution.py:20
  451.2 6.0 %collective-permute-start.58 = (f32[4,6,1,128]{3,2,1,0:T(1,128)S(1)}, f32[4,6,1,128]{3,2,1,0:T(1,128)S(1)}, u32[]{:S(2)}, u32[]{:S(2)}) collective-permute-start(f32[4,6,1,128]{3,2,1,0:T(1,128)S(1)} %get-tuple-element.94), channel_id=1, source_target_pairs={{0,1},{1,2},{2,3},{4,5},{5,6},{6,7},{8,9},{9,10},{10,11},{12,13},{... | collective-permute-start | bytes 36872 | tf_op jit(solution)/shard_map/ppermute | solution.py:20
  460.4 5.7 collective-permute-start.60
  469.2 6.0 %collective-permute-start.62 = (f32[8,6,1,128]{3,2,1,0:T(1,128)S(1)}, f32[8,6,1,128]{3,2,1,0:T(1,128)S(1)}, u32[]{:S(2)}, u32[]{:S(2)}) collective-permute-start(f32[8,6,1,128]{3,2,1,0:T(1,128)S(1)} %get-tuple-element.82), channel_id=1, source_target_pairs={{0,1},{1,2},{2,3},{4,5},{5,6},{6,7},{8,9},{9,10},{10,11},{12,13},{... | collective-permute-start | bytes 73736 | tf_op jit(solution)/shard_map/ppermute | solution.py:20
  477.8 106.1 %all-reduce.21.cloned.1.call-done = f32[4,32,128]{2,1,0:T(8,128)} async-done(((f32[4,32,128]{2,1,0:T(8,128)}), f32[4,32,128]{2,1,0:T(8,128)}) %all-reduce.21.cloned.1.call-update) | async-done | bytes 65552 | tf_op jit(solution)/shard_map/psum | solution.py:99
  (243 shorter events, 157.2 us)
Async XLA Ops:
  6.5 577.4 %all-reduce.21.cloned.1.call-start = ((), (), s32[]{:S(2)}) async-start(), calls=%async_computation | async-start | bytes 131072 | tf_op jit(solution)/shard_map/psum | solution.py:99
  36.5 13.1 %collective-permute-start.1 = (f32[1,1,32,128]{2,1,3,0:T(1,128)S(1)}, f32[1,1,32,128]{2,1,3,0:T(1,128)S(1)}, u32[]{:S(2)}, u32[]{:S(2)}) collective-permute-start(f32[1,1,32,128]{2,1,3,0:T(1,128)S(1)} %get-tuple-element.153), channel_id=1, source_target_pairs={{4,0},{8,4},{12,8},{16,12},{20,16},{24,20},{28,24},{32,28},{36,32}... | collective-permute-start | bytes 49160 | tf_op jit(solution)/shard_map/ppermute | solution.py:23
  37.8 11.8 %collective-permute-start = (f32[1,1,32,128]{2,1,3,0:T(1,128)S(1)}, f32[1,1,32,128]{2,1,3,0:T(1,128)S(1)}, u32[]{:S(2)}, u32[]{:S(2)}) collective-permute-start(f32[1,1,32,128]{2,1,3,0:T(1,128)S(1)} %get-tuple-element.152), channel_id=1, source_target_pairs={{0,4},{4,8},{8,12},{12,16},{16,20},{20,24},{24,28},{28,32},{32,36}... | collective-permute-start | bytes 49160 | tf_op jit(solution)/shard_map/ppermute | solution.py:20
  40.9 41.4 %collective-permute-start.4 = (f32[4,1,32,128]{3,2,1,0:T(8,128)S(1)}, f32[4,1,32,128]{3,2,1,0:T(8,128)S(1)}, u32[]{:S(2)}, u32[]{:S(2)}) collective-permute-start(f32[4,1,32,128]{3,2,1,0:T(8,128)S(1)} %get-tuple-element.151), channel_id=1, source_target_pairs={{0,4},{4,8},{8,12},{12,16},{16,20},{20,24},{24,28},{28,32},{32,36}... | collective-permute-start | bytes 196616 | tf_op jit(solution)/shard_map/ppermute | solution.py:20
  44.8 37.5 %collective-permute-start.5 = (f32[4,1,32,128]{3,2,1,0:T(8,128)S(1)}, f32[4,1,32,128]{3,2,1,0:T(8,128)S(1)}, u32[]{:S(2)}, u32[]{:S(2)}) collective-permute-start(f32[4,1,32,128]{3,2,1,0:T(8,128)S(1)} %get-tuple-element.150), channel_id=1, source_target_pairs={{4,0},{8,4},{12,8},{16,12},{20,16},{24,20},{28,24},{32,28},{36,32}... | collective-permute-start | bytes 196616 | tf_op jit(solution)/shard_map/ppermute | solution.py:23
  50.0 29.9 %collective-permute-start.3 = (f32[1,6,1,128]{2,1,3,0:T(8,128)S(1)}, f32[1,6,1,128]{2,1,3,0:T(8,128)S(1)}, u32[]{:S(2)}, u32[]{:S(2)}) collective-permute-start(f32[1,6,1,128]{2,1,3,0:T(8,128)S(1)} %get-tuple-element.93), channel_id=1, source_target_pairs={{1,0},{2,1},{3,2},{5,4},{6,5},{7,6},{9,8},{10,9},{11,10},{13,12},{... | collective-permute-start | bytes 9224 | tf_op jit(solution)/shard_map/ppermute | solution.py:23
  55.4 24.5 %collective-permute-start.2 = (f32[1,6,1,128]{2,1,3,0:T(8,128)S(1)}, f32[1,6,1,128]{2,1,3,0:T(8,128)S(1)}, u32[]{:S(2)}, u32[]{:S(2)}) collective-permute-start(f32[1,6,1,128]{2,1,3,0:T(8,128)S(1)} %get-tuple-element.92), channel_id=1, source_target_pairs={{0,1},{1,2},{2,3},{4,5},{5,6},{6,7},{8,9},{9,10},{10,11},{12,13},{... | collective-permute-start | bytes 9224 | tf_op jit(solution)/shard_map/ppermute | solution.py:20
  82.3 11.8 %collective-permute-start.7 = (f32[4,6,1,128]{3,2,1,0:T(1,128)S(1)}, f32[4,6,1,128]{3,2,1,0:T(1,128)S(1)}, u32[]{:S(2)}, u32[]{:S(2)}) collective-permute-start(f32[4,6,1,128]{3,2,1,0:T(1,128)S(1)} %get-tuple-element.121), channel_id=1, source_target_pairs={{1,0},{2,1},{3,2},{5,4},{6,5},{7,6},{9,8},{10,9},{11,10},{13,12},{... | collective-permute-start | bytes 36872 | tf_op jit(solution)/shard_map/ppermute | solution.py:23
  84.7 9.4 %collective-permute-start.6 = (f32[4,6,1,128]{3,2,1,0:T(1,128)S(1)}, f32[4,6,1,128]{3,2,1,0:T(1,128)S(1)}, u32[]{:S(2)}, u32[]{:S(2)}) collective-permute-start(f32[4,6,1,128]{3,2,1,0:T(1,128)S(1)} %get-tuple-element.120), channel_id=1, source_target_pairs={{0,1},{1,2},{2,3},{4,5},{5,6},{6,7},{8,9},{9,10},{10,11},{12,13},{... | collective-permute-start | bytes 36872 | tf_op jit(solution)/shard_map/ppermute | solution.py:20
  100.5 8.0 %collective-permute-start.11 = (f32[4,6,1,128]{3,2,1,0:T(1,128)S(1)}, f32[4,6,1,128]{3,2,1,0:T(1,128)S(1)}, u32[]{:S(2)}, u32[]{:S(2)}) collective-permute-start(f32[4,6,1,128]{3,2,1,0:T(1,128)S(1)} %get-tuple-element.119), channel_id=1, source_target_pairs={{1,0},{2,1},{3,2},{5,4},{6,5},{7,6},{9,8},{10,9},{11,10},{13,12},{... | collective-permute-start | bytes 36872 | tf_op jit(solution)/shard_map/ppermute | solution.py:23
  118.2 8.0 %collective-permute-start.15 = (f32[4,6,1,128]{3,2,1,0:T(1,128)S(1)}, f32[4,6,1,128]{3,2,1,0:T(1,128)S(1)}, u32[]{:S(2)}, u32[]{:S(2)}) collective-permute-start(f32[4,6,1,128]{3,2,1,0:T(1,128)S(1)} %get-tuple-element.117), channel_id=1, source_target_pairs={{1,0},{2,1},{3,2},{5,4},{6,5},{7,6},{9,8},{10,9},{11,10},{13,12},{... | collective-permute-start | bytes 36872 | tf_op jit(solution)/shard_map/ppermute | solution.py:23
  136.1 15.5 %collective-permute-start.19 = (f32[4,6,1,128]{3,2,1,0:T(1,128)S(1)}, f32[4,6,1,128]{3,2,1,0:T(1,128)S(1)}, u32[]{:S(2)}, u32[]{:S(2)}) collective-permute-start(f32[4,6,1,128]{3,2,1,0:T(1,128)S(1)} %get-tuple-element.115), channel_id=1, source_target_pairs={{1,0},{2,1},{3,2},{5,4},{6,5},{7,6},{9,8},{10,9},{11,10},{13,12},{... | collective-permute-start | bytes 36872 | tf_op jit(solution)/shard_map/ppermute | solution.py:23
  138.0 13.6 %collective-permute-start.18 = (f32[4,6,1,128]{3,2,1,0:T(1,128)S(1)}, f32[4,6,1,128]{3,2,1,0:T(1,128)S(1)}, u32[]{:S(2)}, u32[]{:S(2)}) collective-permute-start(f32[4,6,1,128]{3,2,1,0:T(1,128)S(1)} %get-tuple-element.114), channel_id=1, source_target_pairs={{0,1},{1,2},{2,3},{4,5},{5,6},{6,7},{8,9},{9,10},{10,11},{12,13},{... | collective-permute-start | bytes 36872 | tf_op jit(solution)/shard_map/ppermute | solution.py:20
  144.7 32.0 %collective-permute-start.32 = (f32[4,1,32,128]{3,2,1,0:T(8,128)}, f32[4,1,32,128]{3,2,1,0:T(8,128)S(1)}, u32[]{:S(2)}, u32[]{:S(2)}) collective-permute-start(f32[4,1,32,128]{3,2,1,0:T(8,128)} %get-tuple-element.137), channel_id=1, source_target_pairs={{0,4},{4,8},{8,12},{12,16},{16,20},{20,24},{24,28},{28,32},{32,36}... | collective-permute-start | bytes 196616 | tf_op jit(solution)/shard_map/ppermute | solution.py:20
  150.2 43.6 %collective-permute-start.33 = (f32[4,1,32,128]{3,2,1,0:T(8,128)}, f32[4,1,32,128]{3,2,1,0:T(8,128)}, u32[]{:S(2)}, u32[]{:S(2)}) collective-permute-start(f32[4,1,32,128]{3,2,1,0:T(8,128)} %get-tuple-element.136), channel_id=1, source_target_pairs={{4,0},{8,4},{12,8},{16,12},{20,16},{24,20},{28,24},{32,28},{36,32}... | collective-permute-start | bytes 196616 | tf_op jit(solution)/shard_map/ppermute | solution.py:23
  160.5 9.8 %collective-permute-start.23 = (f32[4,6,1,128]{3,2,1,0:T(1,128)}, f32[4,6,1,128]{3,2,1,0:T(1,128)}, u32[]{:S(2)}, u32[]{:S(2)}) collective-permute-start(f32[4,6,1,128]{3,2,1,0:T(1,128)} %get-tuple-element.113), channel_id=1, source_target_pairs={{1,0},{2,1},{3,2},{5,4},{6,5},{7,6},{9,8},{10,9},{11,10},{13,12},{... | collective-permute-start | bytes 36872 | tf_op jit(solution)/shard_map/ppermute | solution.py:23
  177.6 8.0 %collective-permute-start.27 = (f32[4,6,1,128]{3,2,1,0:T(1,128)S(1)}, f32[4,6,1,128]{3,2,1,0:T(1,128)S(1)}, u32[]{:S(2)}, u32[]{:S(2)}) collective-permute-start(f32[4,6,1,128]{3,2,1,0:T(1,128)S(1)} %get-tuple-element.111), channel_id=1, source_target_pairs={{1,0},{2,1},{3,2},{5,4},{6,5},{7,6},{9,8},{10,9},{11,10},{13,12},{... | collective-permute-start | bytes 36872 | tf_op jit(solution)/shard_map/ppermute | solution.py:23
  194.7 16.0 %collective-permute-start.31 = (f32[4,6,1,128]{3,2,1,0:T(1,128)S(1)}, f32[4,6,1,128]{3,2,1,0:T(1,128)S(1)}, u32[]{:S(2)}, u32[]{:S(2)}) collective-permute-start(f32[4,6,1,128]{3,2,1,0:T(1,128)S(1)} %get-tuple-element.109), channel_id=1, source_target_pairs={{1,0},{2,1},{3,2},{5,4},{6,5},{7,6},{9,8},{10,9},{11,10},{13,12},{... | collective-permute-start | bytes 36872 | tf_op jit(solution)/shard_map/ppermute | solution.py:23
  196.6 14.0 %collective-permute-start.30 = (f32[4,6,1,128]{3,2,1,0:T(1,128)S(1)}, f32[4,6,1,128]{3,2,1,0:T(1,128)S(1)}, u32[]{:S(2)}, u32[]{:S(2)}) collective-permute-start(f32[4,6,1,128]{3,2,1,0:T(1,128)S(1)} %get-tuple-element.108), channel_id=1, source_target_pairs={{0,1},{1,2},{2,3},{4,5},{5,6},{6,7},{8,9},{9,10},{10,11},{12,13},{... | collective-permute-start | bytes 36872 | tf_op jit(solution)/shard_map/ppermute | solution.py:20
  202.7 154.8 %collective-permute-start.35 = (f32[4,6,1,128]{3,2,1,0:T(1,128)S(1)}, f32[4,6,1,128]{3,2,1,0:T(1,128)S(1)}, u32[]{:S(2)}, u32[]{:S(2)}) collective-permute-start(f32[4,6,1,128]{3,2,1,0:T(1,128)S(1)} %get-tuple-element.107), channel_id=1, source_target_pairs={{1,0},{2,1},{3,2},{5,4},{6,5},{7,6},{9,8},{10,9},{11,10},{13,12},{... | collective-permute-start | bytes 36872 | tf_op jit(solution)/shard_map/ppermute | solution.py:23
  204.6 152.9 %collective-permute-start.34 = (f32[4,6,1,128]{3,2,1,0:T(1,128)S(1)}, f32[4,6,1,128]{3,2,1,0:T(1,128)S(1)}, u32[]{:S(2)}, u32[]{:S(2)}) collective-permute-start(f32[4,6,1,128]{3,2,1,0:T(1,128)S(1)} %get-tuple-element.106), channel_id=1, source_target_pairs={{0,1},{1,2},{2,3},{4,5},{5,6},{6,7},{8,9},{9,10},{10,11},{12,13},{... | collective-permute-start | bytes 36872 | tf_op jit(solution)/shard_map/ppermute | solution.py:20
  396.6 8.2 %collective-permute-start.47 = (f32[4,6,1,128]{3,2,1,0:T(1,128)S(1)}, f32[4,6,1,128]{3,2,1,0:T(1,128)S(1)}, u32[]{:S(2)}, u32[]{:S(2)}) collective-permute-start(f32[4,6,1,128]{3,2,1,0:T(1,128)S(1)} %get-tuple-element.101), channel_id=1, source_target_pairs={{1,0},{2,1},{3,2},{5,4},{6,5},{7,6},{9,8},{10,9},{11,10},{13,12},{... | collective-permute-start | bytes 36872 | tf_op jit(solution)/shard_map/ppermute | solution.py:23
  414.3 8.0 %collective-permute-start.51 = (f32[4,6,1,128]{3,2,1,0:T(1,128)S(1)}, f32[4,6,1,128]{3,2,1,0:T(1,128)S(1)}, u32[]{:S(2)}, u32[]{:S(2)}) collective-permute-start(f32[4,6,1,128]{3,2,1,0:T(1,128)S(1)} %get-tuple-element.99), channel_id=1, source_target_pairs={{1,0},{2,1},{3,2},{5,4},{6,5},{7,6},{9,8},{10,9},{11,10},{13,12},{... | collective-permute-start | bytes 36872 | tf_op jit(solution)/shard_map/ppermute | solution.py:23
  467.2 8.8 %collective-permute-start.63 = (f32[8,6,1,128]{3,2,1,0:T(1,128)S(1)}, f32[8,6,1,128]{3,2,1,0:T(1,128)S(1)}, u32[]{:S(2)}, u32[]{:S(2)}) collective-permute-start(f32[8,6,1,128]{3,2,1,0:T(1,128)S(1)} %get-tuple-element.83), channel_id=1, source_target_pairs={{1,0},{2,1},{3,2},{5,4},{6,5},{7,6},{9,8},{10,9},{11,10},{13,12},{... | collective-permute-start | bytes 73736 | tf_op jit(solution)/shard_map/ppermute | solution.py:23
  (62 other events, 980.0 us)
Sparse Core Ops, SparseCore 0:
  477.9 105.9 all-reduce.20
where the time goes:
time: 595 us; the launch traced here: 592 us
  starting transfers between devices  224 us (38%)
  blocking collectives  174 us (29%)
  waiting for transfers between devices  153 us (26%)
  other arithmetic  15 us (3%)
  between operations  14.6 us (2%)
  local copies, waits for them, and re-layouts  12.1 us (2%)
    ppermute x32, starting transfers between devices, padded_2(): lax.ppermute(lax.slice_in_dim(block, block.shape[dim] - width, None, axis...  166 us
    psum x1, blocking collectives, body(): predicted = lax.psum(local_values, ('gx', 'gy'))  145 us
    psum x1, waiting for transfers between devices, reduce_groups(): summed = lax.psum(partial_value, 'src')  106 us
    ppermute x32, starting transfers between devices, padded_2(): lax.ppermute(lax.slice_in_dim(block, 0, width, axis=dim), axis, backward)  58.2 us
    all_gather x1, blocking collectives, body(): panel = lax.all_gather(conductivity, 'src', axis=2, tiled=True)  29 us
    ppermute x32, waiting for transfers between devices, padded_2(): lax.ppermute(lax.slice_in_dim(block, block.shape[dim] - width, None, axis...  24.7 us
    ppermute x32, waiting for transfers between devices, padded_2(): lax.ppermute(lax.slice_in_dim(block, 0, width, axis=dim), axis, backward)  22 us
  transfers between devices with their start and end apart: 65, of which 24 were waited for; matrix products, arithmetic and copies ran while one was open for 3% of the time, Pallas kernels for 0%

commit v1 on v0

--- a/solution.py
+++ b/solution.py
@@ -101,7 +101,10 @@
 
 
 def body(warm_potential, warm_adjoint, conductivity, electrodes, receivers, observed, source_order):
-    panel = lax.all_gather(conductivity, "src", axis=2, tiled=True)
+    fields = []
+    for _ in range(lax.psum(1, "src")):
+        fields.append(conductivity)
+    panel = jnp.concatenate(lax.all_to_all(jnp.stack(fields, axis=0), "src", 0, 0), 2)
     group = lax.axis_index("src")
     slots = warm_potential.shape[0]
     width_x = panel.shape[0]

time: 595 us -> 564 us (0.948)
  blocking collectives: 174 us -> 138 us
  waiting for transfers between devices: 153 us -> 186 us
  starting transfers between devices: 224 us -> 194 us
    ppermute x32, starting transfers between devices: 166 us -> 102 us  [padded_2(): lax.ppermute(lax.slice_in_dim(block, block.shape[dim] - width, None, axis...]
    ppermute x32, waiting for transfers between devices: 22 us -> 80.4 us  [padded_2(): lax.ppermute(lax.slice_in_dim(block, 0, width, axis=dim), axis, backward)]
    all_gather x1 -> x0, blocking collectives: 29 us -> none  [body(): panel = lax.all_gather(conductivity, 'src', axis=2, tiled=True)]
    ppermute x32, starting transfers between devices: 58.2 us -> 87.3 us  [padded_2(): lax.ppermute(lax.slice_in_dim(block, 0, width, axis=dim), axis, backward)]
    psum x1, waiting for transfers between devices: 106 us -> 90.8 us  [reduce_groups(): summed = lax.psum(partial_value, 'src')]
    ppermute x32, waiting for transfers between devices: 24.7 us -> 14.8 us  [padded_2(): lax.ppermute(lax.slice_in_dim(block, block.shape[dim] - width, None, axis...]
    psum x1, blocking collectives: 145 us -> 138 us  [body(): predicted = lax.psum(local_values, ('gx', 'gy'))]
  transfers between devices with their start and end apart: 65 -> 66, of which waited for: 24 -> 28; matrix products, arithmetic and copies ran while one was open for 3% -> 2% of each run, Pallas kernels for 0% -> 0%
where the time goes in v1:
time: 564 us; the launch traced here: 561 us
  starting transfers between devices  194 us (34%)
  waiting for transfers between devices  186 us (33%)
  blocking collectives  138 us (24%)
  between operations  14.7 us (3%)
  local copies, waits for them, and re-layouts  14.6 us (3%)
  other arithmetic  12.8 us (2%)
    psum x1, blocking collectives, body(): predicted = lax.psum(local_values, ('gx', 'gy'))  138 us
    ppermute x32, starting transfers between devices, padded_2(): lax.ppermute(lax.slice_in_dim(block, block.shape[dim] - width, None, axis...  102 us
    psum x1, waiting for transfers between devices, reduce_groups(): summed = lax.psum(partial_value, 'src')  90.8 us
    ppermute x32, starting transfers between devices, padded_2(): lax.ppermute(lax.slice_in_dim(block, 0, width, axis=dim), axis, backward)  87.3 us
    ppermute x32, waiting for transfers between devices, padded_2(): lax.ppermute(lax.slice_in_dim(block, 0, width, axis=dim), axis, backward)  80.4 us
    ppermute x32, waiting for transfers between devices, padded_2(): lax.ppermute(lax.slice_in_dim(block, block.shape[dim] - width, None, axis...  14.8 us
  transfers between devices with their start and end apart: 66, of which 28 were waited for; matrix products, arithmetic and copies ran while one was open for 2% of the time, Pallas kernels for 0%

profile of v1, /device:TPU:16, one launch (start us, length us, event | category | flops | bytes accessed | tf_op | source)
XLA Modules:
  0.0 561.4 jit_solution(571138566933516642)
XLA Ops:
  8.1 5.3 all-to-all-start
  22.1 5.2 collective-permute-start
  28.7 4.8 collective-permute-start.6
  35.7 6.0 %collective-permute-start.2 = (f32[1,6,1,128]{2,3,1,0:T(8,128)S(1)}, f32[1,6,1,128]{2,3,1,0:T(8,128)S(1)}, u32[]{:S(2)}, u32[]{:S(2)}) collective-permute-start(f32[1,6,1,128]{2,3,1,0:T(8,128)S(1)} %get-tuple-element.124), channel_id=1, source_target_pairs={{0,1},{1,2},{2,3},{4,5},{5,6},{6,7},{8,9},{9,10},{10,11},{12,13},{... | collective-permute-start | bytes 9224 | tf_op jit(solution)/shard_map/ppermute | solution.py:20
  43.9 14.7 %collective-permute-done.2 = f32[1,6,1,128]{2,3,1,0:T(8,128)S(1)} collective-permute-done((f32[1,6,1,128]{2,3,1,0:T(8,128)S(1)}, f32[1,6,1,128]{2,3,1,0:T(8,128)S(1)}, u32[]{:S(2)}, u32[]{:S(2)}) %collective-permute-start.2) | collective-permute-done | bytes 3104 | tf_op jit(solution)/shard_map/ppermute | solution.py:20
  58.7 5.4 collective-permute-done.3
  72.3 4.8 collective-permute-done.9
  97.0 4.8 collective-permute-start.15
  115.0 4.8 collective-permute-start.19
  120.5 4.9 collective-permute-start.32
  157.4 4.8 collective-permute-start.27
  176.0 4.8 collective-permute-start.31
  189.2 138.5 %psum.14 = f32[4,128]{1,0:T(4,128)S(1)} all-reduce(f32[4,128]{1,0:T(4,128)S(1)} %fusion.304), channel_id=1, replica_groups=mesh['src'=8,'gx'=16,'gy'=4] {'gx','gy'}, use_global_device_ids=true, to_apply=%region_0.1 | all-reduce | flops 512 | bytes 4096 | tf_op jit(solution)/shard_map/psum | solution.py:143
  351.9 4.8 collective-permute-start.43
  364.5 7.7 %collective-permute-done.45 = f32[4,1,32,128]{3,2,1,0:T(8,128)S(1)} collective-permute-done((f32[4,1,32,128]{3,2,1,0:T(8,128)S(1)}, f32[4,1,32,128]{3,2,1,0:T(8,128)S(1)}, u32[]{:S(2)}, u32[]{:S(2)}) %collective-permute-start.45) | collective-permute-done | bytes 65568 | tf_op jit(solution)/shard_map/ppermute | solution.py:23
  374.1 4.8 collective-permute-start.47
  382.1 7.3 %collective-permute-start.48 = (f32[4,1,32,128]{3,2,1,0:T(8,128)S(1)}, f32[4,1,32,128]{3,2,1,0:T(8,128)S(1)}, u32[]{:S(2)}, u32[]{:S(2)}) collective-permute-start(f32[4,1,32,128]{3,2,1,0:T(8,128)S(1)} %get-tuple-element.130), channel_id=1, source_target_pairs={{0,4},{4,8},{8,12},{12,16},{16,20},{20,24},{24,28},{28,32},{32,36}... | collective-permute-start | bytes 196616 | tf_op jit(solution)/shard_map/ppermute | solution.py:20
  396.9 5.0 collective-permute-start.51
  415.5 4.8 collective-permute-start.55
  423.6 5.1 collective-permute-start.56
  434.3 4.8 collective-permute-start.59
  442.5 4.9 collective-permute-start.60
  453.2 4.8 collective-permute-start.63
  462.2 90.8 %all-reduce.21.cloned.1.call-done = f32[4,32,128]{2,1,0:T(8,128)} async-done(((f32[4,32,128]{2,1,0:T(8,128)}), f32[4,32,128]{2,1,0:T(8,128)}) %all-reduce.21.cloned.1.call-update) | async-done | bytes 65552 | tf_op jit(solution)/shard_map/psum | solution.py:99
  (253 shorter events, 192.9 us)
Async XLA Ops:
  8.1 12.5 %all-to-all-start = ((f32[8,1,2048]{2,1,0:T(1,128)}), f32[8,1,2048]{2,1,0:T(1,128)S(1)}, u32[]{:S(2)}, u32[]{:S(2)}) async-start(f32[8,1,2048]{2,1,0:T(1,128)} %reshape.188), calls=%async_computation | async-start | bytes 131072 | tf_op jit(solution)/shard_map/all_to_all | solution.py:107
  13.4 539.5 %all-reduce.21.cloned.1.call-start = ((), (), s32[]{:S(2)}) async-start(), calls=%async_computation.1 | async-start | bytes 131072 | tf_op jit(solution)/shard_map/psum | solution.py:99
  22.1 13.4 %collective-permute-start = (f32[1,1,32,128]{2,3,1,0:T(8,128)S(1)}, f32[1,1,32,128]{2,3,1,0:T(8,128)S(1)}, u32[]{:S(2)}, u32[]{:S(2)}) collective-permute-start(f32[1,1,32,128]{2,3,1,0:T(8,128)S(1)} %get-tuple-element.156), channel_id=1, source_target_pairs={{0,4},{4,8},{8,12},{12,16},{16,20},{20,24},{24,28},{28,32},{32,36}... | collective-permute-start | bytes 49160 | tf_op jit(solution)/shard_map/ppermute | solution.py:20
  27.4 8.1 %collective-permute-start.1 = (f32[1,1,32,128]{2,3,1,0:T(8,128)S(1)}, f32[1,1,32,128]{2,3,1,0:T(8,128)S(1)}, u32[]{:S(2)}, u32[]{:S(2)}) collective-permute-start(f32[1,1,32,128]{2,3,1,0:T(8,128)S(1)} %get-tuple-element.157), channel_id=1, source_target_pairs={{4,0},{8,4},{12,8},{16,12},{20,16},{24,20},{28,24},{32,28},{36,32}... | collective-permute-start | bytes 49160 | tf_op jit(solution)/shard_map/ppermute | solution.py:23
  28.7 38.9 %collective-permute-start.6 = (f32[4,6,1,128]{3,2,1,0:T(1,128)S(1)}, f32[4,6,1,128]{3,2,1,0:T(1,128)S(1)}, u32[]{:S(2)}, u32[]{:S(2)}) collective-permute-start(f32[4,6,1,128]{3,2,1,0:T(1,128)S(1)} %get-tuple-element.122), channel_id=1, source_target_pairs={{0,1},{1,2},{2,3},{4,5},{5,6},{6,7},{8,9},{9,10},{10,11},{12,13},{... | collective-permute-start | bytes 36872 | tf_op jit(solution)/shard_map/ppermute | solution.py:20
  33.5 34.1 %collective-permute-start.7 = (f32[4,6,1,128]{3,2,1,0:T(1,128)S(1)}, f32[4,6,1,128]{3,2,1,0:T(1,128)S(1)}, u32[]{:S(2)}, u32[]{:S(2)}) collective-permute-start(f32[4,6,1,128]{3,2,1,0:T(1,128)S(1)} %get-tuple-element.123), channel_id=1, source_target_pairs={{1,0},{2,1},{3,2},{5,4},{6,5},{7,6},{9,8},{10,9},{11,10},{13,12},{... | collective-permute-start | bytes 36872 | tf_op jit(solution)/shard_map/ppermute | solution.py:23
  35.7 22.9 %collective-permute-start.2 = (f32[1,6,1,128]{2,3,1,0:T(8,128)S(1)}, f32[1,6,1,128]{2,3,1,0:T(8,128)S(1)}, u32[]{:S(2)}, u32[]{:S(2)}) collective-permute-start(f32[1,6,1,128]{2,3,1,0:T(8,128)S(1)} %get-tuple-element.124), channel_id=1, source_target_pairs={{0,1},{1,2},{2,3},{4,5},{5,6},{6,7},{8,9},{9,10},{10,11},{12,13},{... | collective-permute-start | bytes 9224 | tf_op jit(solution)/shard_map/ppermute | solution.py:20
  41.8 22.3 %collective-permute-start.3 = (f32[1,6,1,128]{2,3,1,0:T(8,128)S(1)}, f32[1,6,1,128]{2,3,1,0:T(8,128)S(1)}, u32[]{:S(2)}, u32[]{:S(2)}) collective-permute-start(f32[1,6,1,128]{2,3,1,0:T(8,128)S(1)} %get-tuple-element.125), channel_id=1, source_target_pairs={{1,0},{2,1},{3,2},{5,4},{6,5},{7,6},{9,8},{10,9},{11,10},{13,12},{... | collective-permute-start | bytes 9224 | tf_op jit(solution)/shard_map/ppermute | solution.py:23
  79.6 7.7 %collective-permute-start.11 = (f32[4,6,1,128]{3,2,1,0:T(1,128)S(1)}, f32[4,6,1,128]{3,2,1,0:T(1,128)S(1)}, u32[]{:S(2)}, u32[]{:S(2)}) collective-permute-start(f32[4,6,1,128]{3,2,1,0:T(1,128)S(1)} %get-tuple-element.121), channel_id=1, source_target_pairs={{1,0},{2,1},{3,2},{5,4},{6,5},{7,6},{9,8},{10,9},{11,10},{13,12},{... | collective-permute-start | bytes 36872 | tf_op jit(solution)/shard_map/ppermute | solution.py:23
  97.0 7.7 %collective-permute-start.15 = (f32[4,6,1,128]{3,2,1,0:T(1,128)S(1)}, f32[4,6,1,128]{3,2,1,0:T(1,128)S(1)}, u32[]{:S(2)}, u32[]{:S(2)}) collective-permute-start(f32[4,6,1,128]{3,2,1,0:T(1,128)S(1)} %get-tuple-element.119), channel_id=1, source_target_pairs={{1,0},{2,1},{3,2},{5,4},{6,5},{7,6},{9,8},{10,9},{11,10},{13,12},{... | collective-permute-start | bytes 36872 | tf_op jit(solution)/shard_map/ppermute | solution.py:23
  113.0 13.7 %collective-permute-start.18 = (f32[4,6,1,128]{3,2,1,0:T(1,128)S(1)}, f32[4,6,1,128]{3,2,1,0:T(1,128)S(1)}, u32[]{:S(2)}, u32[]{:S(2)}) collective-permute-start(f32[4,6,1,128]{3,2,1,0:T(1,128)S(1)} %get-tuple-element.116), channel_id=1, source_target_pairs={{0,1},{1,2},{2,3},{4,5},{5,6},{6,7},{8,9},{9,10},{10,11},{12,13},{... | collective-permute-start | bytes 36872 | tf_op jit(solution)/shard_map/ppermute | solution.py:20
  115.0 11.8 %collective-permute-start.19 = (f32[4,6,1,128]{3,2,1,0:T(1,128)S(1)}, f32[4,6,1,128]{3,2,1,0:T(1,128)S(1)}, u32[]{:S(2)}, u32[]{:S(2)}) collective-permute-start(f32[4,6,1,128]{3,2,1,0:T(1,128)S(1)} %get-tuple-element.117), channel_id=1, source_target_pairs={{1,0},{2,1},{3,2},{5,4},{6,5},{7,6},{9,8},{10,9},{11,10},{13,12},{... | collective-permute-start | bytes 36872 | tf_op jit(solution)/shard_map/ppermute | solution.py:23
  120.5 31.0 %collective-permute-start.32 = (f32[4,1,32,128]{3,2,1,0:T(8,128)}, f32[4,1,32,128]{3,2,1,0:T(8,128)}, u32[]{:S(2)}, u32[]{:S(2)}) collective-permute-start(f32[4,1,32,128]{3,2,1,0:T(8,128)} %get-tuple-element.139), channel_id=1, source_target_pairs={{0,4},{4,8},{8,12},{12,16},{16,20},{20,24},{24,28},{28,32},{32,36}... | collective-permute-start | bytes 196616 | tf_op jit(solution)/shard_map/ppermute | solution.py:20
  125.4 45.0 %collective-permute-start.33 = (f32[4,1,32,128]{3,2,1,0:T(8,128)}, f32[4,1,32,128]{3,2,1,0:T(8,128)}, u32[]{:S(2)}, u32[]{:S(2)}) collective-permute-start(f32[4,1,32,128]{3,2,1,0:T(8,128)} %get-tuple-element.138), channel_id=1, source_target_pairs={{4,0},{8,4},{12,8},{16,12},{20,16},{24,20},{28,24},{32,28},{36,32}... | collective-permute-start | bytes 196616 | tf_op jit(solution)/shard_map/ppermute | solution.py:23
  135.2 8.0 %collective-permute-start.22 = (f32[4,6,1,128]{3,2,1,0:T(1,128)}, f32[4,6,1,128]{3,2,1,0:T(1,128)S(1)}, u32[]{:S(2)}, u32[]{:S(2)}) collective-permute-start(f32[4,6,1,128]{3,2,1,0:T(1,128)} %get-tuple-element.114), channel_id=1, source_target_pairs={{0,1},{1,2},{2,3},{4,5},{5,6},{6,7},{8,9},{9,10},{10,11},{12,13},{... | collective-permute-start | bytes 36872 | tf_op jit(solution)/shard_map/ppermute | solution.py:20
  138.6 7.9 %collective-permute-start.23 = (f32[4,6,1,128]{3,2,1,0:T(1,128)}, f32[4,6,1,128]{3,2,1,0:T(1,128)S(1)}, u32[]{:S(2)}, u32[]{:S(2)}) collective-permute-start(f32[4,6,1,128]{3,2,1,0:T(1,128)} %get-tuple-element.115), channel_id=1, source_target_pairs={{1,0},{2,1},{3,2},{5,4},{6,5},{7,6},{9,8},{10,9},{11,10},{13,12},{... | collective-permute-start | bytes 36872 | tf_op jit(solution)/shard_map/ppermute | solution.py:23
  174.1 13.5 %collective-permute-start.30 = (f32[4,6,1,128]{3,2,1,0:T(1,128)S(1)}, f32[4,6,1,128]{3,2,1,0:T(1,128)S(1)}, u32[]{:S(2)}, u32[]{:S(2)}) collective-permute-start(f32[4,6,1,128]{3,2,1,0:T(1,128)S(1)} %get-tuple-element.110), channel_id=1, source_target_pairs={{0,1},{1,2},{2,3},{4,5},{5,6},{6,7},{8,9},{9,10},{10,11},{12,13},{... | collective-permute-start | bytes 36872 | tf_op jit(solution)/shard_map/ppermute | solution.py:20
  176.0 11.6 %collective-permute-start.31 = (f32[4,6,1,128]{3,2,1,0:T(1,128)S(1)}, f32[4,6,1,128]{3,2,1,0:T(1,128)S(1)}, u32[]{:S(2)}, u32[]{:S(2)}) collective-permute-start(f32[4,6,1,128]{3,2,1,0:T(1,128)S(1)} %get-tuple-element.111), channel_id=1, source_target_pairs={{1,0},{2,1},{3,2},{5,4},{6,5},{7,6},{9,8},{10,9},{11,10},{13,12},{... | collective-permute-start | bytes 36872 | tf_op jit(solution)/shard_map/ppermute | solution.py:23
  180.8 147.4 %collective-permute-start.34 = (f32[4,6,1,128]{3,2,1,0:T(1,128)S(1)}, f32[4,6,1,128]{3,2,1,0:T(1,128)S(1)}, u32[]{:S(2)}, u32[]{:S(2)}) collective-permute-start(f32[4,6,1,128]{3,2,1,0:T(1,128)S(1)} %get-tuple-element.108), channel_id=1, source_target_pairs={{0,1},{1,2},{2,3},{4,5},{5,6},{6,7},{8,9},{9,10},{10,11},{12,13},{... | collective-permute-start | bytes 36872 | tf_op jit(solution)/shard_map/ppermute | solution.py:20
  184.0 144.3 %collective-permute-start.35 = (f32[4,6,1,128]{3,2,1,0:T(1,128)S(1)}, f32[4,6,1,128]{3,2,1,0:T(1,128)S(1)}, u32[]{:S(2)}, u32[]{:S(2)}) collective-permute-start(f32[4,6,1,128]{3,2,1,0:T(1,128)S(1)} %get-tuple-element.109), channel_id=1, source_target_pairs={{1,0},{2,1},{3,2},{5,4},{6,5},{7,6},{9,8},{10,9},{11,10},{13,12},{... | collective-permute-start | bytes 36872 | tf_op jit(solution)/shard_map/ppermute | solution.py:23
  363.2 9.0 %collective-permute-start.45 = (f32[4,1,32,128]{3,2,1,0:T(8,128)S(1)}, f32[4,1,32,128]{3,2,1,0:T(8,128)S(1)}, u32[]{:S(2)}, u32[]{:S(2)}) collective-permute-start(f32[4,1,32,128]{3,2,1,0:T(8,128)S(1)} %get-tuple-element.133), channel_id=1, source_target_pairs={{4,0},{8,4},{12,8},{16,12},{20,16},{24,20},{28,24},{32,28},{36,32}... | collective-permute-start | bytes 196616 | tf_op jit(solution)/shard_map/ppermute | solution.py:23
  382.1 8.6 %collective-permute-start.48 = (f32[4,1,32,128]{3,2,1,0:T(8,128)S(1)}, f32[4,1,32,128]{3,2,1,0:T(8,128)S(1)}, u32[]{:S(2)}, u32[]{:S(2)}) collective-permute-start(f32[4,1,32,128]{3,2,1,0:T(8,128)S(1)} %get-tuple-element.130), channel_id=1, source_target_pairs={{0,4},{4,8},{8,12},{12,16},{16,20},{20,24},{24,28},{28,32},{32,36}... | collective-permute-start | bytes 196616 | tf_op jit(solution)/shard_map/ppermute | solution.py:20
  451.3 8.2 %collective-permute-start.62 = (f32[8,6,1,128]{3,2,1,0:T(1,128)S(1)}, f32[8,6,1,128]{3,2,1,0:T(1,128)S(1)}, u32[]{:S(2)}, u32[]{:S(2)}) collective-permute-start(f32[8,6,1,128]{3,2,1,0:T(1,128)S(1)} %get-tuple-element.86), channel_id=1, source_target_pairs={{0,1},{1,2},{2,3},{4,5},{5,6},{6,7},{8,9},{9,10},{10,11},{12,13},{... | collective-permute-start | bytes 73736 | tf_op jit(solution)/shard_map/ppermute | solution.py:20
  453.2 7.8 %collective-permute-start.63 = (f32[8,6,1,128]{3,2,1,0:T(1,128)S(1)}, f32[8,6,1,128]{3,2,1,0:T(1,128)S(1)}, u32[]{:S(2)}, u32[]{:S(2)}) collective-permute-start(f32[8,6,1,128]{3,2,1,0:T(1,128)S(1)} %get-tuple-element.87), channel_id=1, source_target_pairs={{1,0},{2,1},{3,2},{5,4},{6,5},{7,6},{9,8},{10,9},{11,10},{13,12},{... | collective-permute-start | bytes 73736 | tf_op jit(solution)/shard_map/ppermute | solution.py:23
  (64 other events, 609.0 us)
Sparse Core Ops, SparseCore 0:
  462.3 90.6 all-reduce.20
